TPU v7x, 256 devices: a whole 4x4x8 slice. The times are simulated.
256 devices in a mesh: lat: 4 (over x_lo, core), lon: 64 (over z, x_hi, y).
Axes of the slice: x: 4 (x_hi: 2, x_lo: 2; x = x_hi * 2 + x_lo), y: 4, z: 8, core: 2. Of those that a mesh axis runs over, the one named last changes fastest.
Arguments:
- pre_act: bfloat16 [8, 49152, 512], P('lat', 'lon'), may hold values from -18 to 18
- grad_out: bfloat16 [8, 49152, 512], P('lat', 'lon'), may hold values from -61 to 61
- kernel: bfloat16 [3, 3, 512, 512], replicated, may hold values from -0.09375 to 0.09375
Outputs:
- grad_in: bfloat16 [8, 49152, 512], P('lat', 'lon')
- grad_kernel: float32 [512, 3, 3, 512], P('lon', None, None, 'lat')
All inputs are finite; a program needn't handle non-finite values.
Results may differ from a plain program's by a relative error of at most 0.0028.
Values may be sent and summed in bfloat16 or wider, within the bound.
A program may use at most 128 MiB of HBM per device.

v0:
```python
import jax
import jax.numpy as jnp
from jax import lax
from jax.sharding import PartitionSpec as P


def extended(shard, sides, width, wrap):
    for axis, dim in sides:
        size, length = (lax.axis_size(axis), shard.shape[dim])
        up = [(i, (i + 1) % size) for i in range(size if wrap else size - 1)]
        down = [(j, i) for i, j in up]
        last = lax.slice_in_dim(shard, length - width, length, axis=dim)
        first = lax.slice_in_dim(shard, 0, width, axis=dim)
        before = lax.ppermute(last, axis, up)
        after = lax.ppermute(first, axis, down)
        shard = jnp.concatenate([before, shard, after], axis=dim)
    return shard


def extend(field):
    widened = extended(field, (("lon", 1),), 1, True)
    return extended(widened, (("lat", 0),), 1, False)


def shifted_list(padded, height, breadth, channels):
    pieces = []
    for lat_off in (-1, 0, 1):
        for lon_off in (-1, 0, 1):
            window = padded[1 - lat_off : 1 - lat_off + height, 1 - lon_off : 1 - lon_off + breadth]
            pieces.append(window.reshape(-1, channels))
    return pieces


def transposed_conv(pieces, kernel):
    running = None
    position = 0
    for lat_pos in range(3):
        for lon_pos in range(3):
            product = lax.dot_general(
                pieces[position],
                kernel[lat_pos, lon_pos],
                (((1,), (1,)), ((), ())),
                preferred_element_type=jnp.float32,
            )
            running = product if running is None else running + product
            position = position + 1
    return running


def shards(pre_act, grad_out, kernel):
    height, breadth, channels = pre_act.shape
    pre_wide = pre_act.astype(jnp.float32).reshape(-1, channels)
    activated = jax.nn.silu(pre_wide).astype(jnp.bfloat16)
    pieces = shifted_list(extend(grad_out), height, breadth, channels)
    blocks = []
    for shifted in pieces:
        blocks.append(
            lax.dot_general(
                shifted, activated, (((0,), (0,)), ((), ())), preferred_element_type=jnp.float32
            )
        )
    lon_partial = lax.psum_scatter(
        jnp.stack(blocks, axis=1).reshape(
            channels // lax.axis_size("lon") * lax.axis_size("lon"), 3, 3, channels
        ),
        "lon",
        scatter_dimension=0,
        tiled=True,
    )
    summed = lax.psum_scatter(lon_partial, "lat", scatter_dimension=3, tiled=True)
    grad_act = transposed_conv(pieces, kernel)
    sigmoid_pre = jax.nn.sigmoid(pre_wide)
    grad_in = (grad_act * sigmoid_pre * (1.0 + pre_wide * (1.0 - sigmoid_pre))).astype(jnp.bfloat16)
    local_squares = jnp.sum(summed * summed)
    grand_total = lax.psum(local_squares, ("lat", "lon"))
    factor = jnp.float32(3.0 * channels) / jnp.sqrt(grand_total + 1e-06)
    return (grad_in.reshape(height, breadth, channels), factor * summed)


def solution(mesh):
    in_specs = (P("lat", "lon", None), P("lat", "lon", None), P())
    out_specs = (P("lat", "lon", None), P("lon", None, None, "lat"))
    return jax.shard_map(shards, mesh=mesh, in_specs=in_specs, out_specs=out_specs, check_vma=False)
```

profile of v0, /device:TPU:1, one launch (start us, length us, event | category | flops | bytes accessed | tf_op | source)
XLA Modules:
  0.0 560.9 jit_solution(11889228804684524888)
XLA Ops:
  7.2 0.0 reduce-scatter.3.cloned.1.call-start
  7.2 0.7 fusion.57
  8.0 0.2 copy.27
  8.2 2.2 collective-permute-start
  10.4 0.2 copy.28
  10.6 9.3 %collective-permute-start.1 = (bf16[2,1,512]{1,2,0:T(8,128)(2,1)S(1)}, bf16[2,1,512]{1,2,0:T(8,128)(2,1)S(1)}, u32[]{:S(2)}, u32[]{:S(2)}) collective-permute-start(bf16[2,1,512]{1,2,0:T(8,128)(2,1)S(1)} %copy.28), channel_id=1, source_target_pairs={{1,0},{2,1},{3,2},{4,3},{5,4},{6,5},{7,6},{8,7},{9,8},{10,9},{11,1... | collective-permute-start | bytes 6152 | tf_op jit(solution)/shard_map/ppermute | solution.py:15
  19.9 1.7 copy.29
  21.6 4.0 collective-permute-done
  25.6 0.7 copy-done.14
  26.3 0.7 copy-done.16
  27.0 1.0 pad_maximum_fusion.1
  28.1 0.1 fusion.56
  28.2 1.2 copy.30
  29.4 3.1 collective-permute-start.2
  32.6 1.2 copy.39
  33.8 2.5 collective-permute-start.3
  36.4 4.1 pad_maximum_fusion.2
  40.5 2.6 collective-permute-done.2
  43.1 2.2 copy.31
  45.3 0.3 collective-permute-done.3
  45.7 2.2 copy.40
  47.9 4.6 maximum_maximum_fusion
  52.5 1.5 fusion.19
  54.0 1.5 fusion.18
  55.5 0.0 copy-start.13
  55.5 1.1 fusion.17
  56.6 0.3 copy-done.13
  56.9 1.1 fusion.16
  58.0 0.3 copy-done.5
  58.3 1.3 fusion.15
  59.7 1.1 fusion.14
  60.8 1.5 fusion.13
  62.3 1.5 fusion.12
  63.8 1.1 fusion.11
  64.9 3.6 copy-done.4
  68.5 0.0 reduce-scatter.3.cloned.1.call-update
  68.5 0.3 reduce-scatter.5.cloned.1.call-start
  68.8 1.1 copy-done.18
  69.9 3.7 fusion.8
  73.6 2.7 copy.36
  76.3 2.6 copy.38
  78.9 6.9 %fusion.54 = (bf16[2,768,512]{1,2,0:T(8,128)(2,1)}, bf16[2,768,512]{1,2,0:T(8,128)(2,1)}, bf16[2,768,512]{1,2,0:T(8,128)(2,1)}, bf16[2,768,512]{1,2,0:T(8,128)(2...) fusion(bf16[3,770,512]{1,2,0:T(8,128)(2,1)S(1)} %copy-done.1, bf16[3,770,512]{1,2,0:T(8,128)(2,1)} %copy-done.2), kind=kLoop, calls=%fused_computation.73 | loop fusion | bytes 18874368 | tf_op jit(solution)/shard_map/slice | solution.py:29
  85.9 1.8 copy.32
  87.7 2.6 copy.33
  90.3 1.6 copy.34
  91.9 1.7 copy.41
  93.6 2.6 copy.42
  96.3 2.6 copy.43
  98.9 2.2 fusion.28
  101.1 2.2 convolution_add_fusion.7
  103.3 2.2 convolution_add_fusion.6
  105.5 0.0 copy-start.6
  105.5 2.2 convolution_add_fusion.5
  107.7 2.2 convolution_add_fusion.4
  109.9 2.1 convolution_add_fusion.3
  111.9 3.7 convolution_add_fusion.2
  115.7 289.8 %reduce-scatter.3.cloned.1.call-done = f32[8,3,3,512]{3,0,2,1:T(8,128)} async-done(((f32[512,3,3,512]{3,0,2,1:T(8,128)}), f32[8,3,3,512]{3,0,2,1:T(8,128)}) %reduce-scatter.3.cloned.1.call-update) | async-done | bytes 147472 | tf_op jit(solution)/shard_map/reduce_scatter | solution.py:62
  405.5 0.0 reduce-scatter.5.cloned.1.call-update
  405.5 5.4 convolution_add_fusion.1
  410.9 57.7 %reduce-scatter.5.cloned.1.call-done = f32[8,3,3,128]{3,0,2,1:T(8,128)} async-done(((f32[8,3,3,512]{3,0,2,1:T(8,128)}), f32[8,3,3,128]{3,0,2,1:T(8,128)}) %reduce-scatter.5.cloned.1.call-update) | async-done | bytes 36880 | tf_op jit(solution)/shard_map/reduce_scatter | solution.py:70
  468.7 1.4 multiply_reduce_fusion
  470.0 5.7 %fusion.10 = bf16[1536,512]{1,0:T(8,128)(2,1)} fusion(f32[1536,512]{1,0:T(8,128)} %get-tuple-element.17, f32[1536,512]{1,0:T(8,128)S(1)} %copy-done.3, f32[1536,512]{1,0:T(8,128)} %convolution_add_fusion.1, bf16[1536,512]{1,0:T(8,128)(2,1)} %bitcast.114, bf16[3,3,512,512]{3,2,1,0:T(8,128)(2,1)} %param.5), kind=kOutput, calls=%fused_computation.22 | convolution fusion | flops 808452096 | bytes 13107200 | tf_op jit(solution)/shard_map/dot_general | solution.py:39
  475.7 77.0 %psum.7 = f32[]{:T(128)} all-reduce(f32[]{:T(128)} %multiply_reduce_fusion), channel_id=1, replica_groups=mesh['lat'=4,'lon'=64] {'lat','lon'}, use_global_device_ids=true, to_apply=%region_3.4 | all-reduce | flops 1 | bytes 8 | tf_op jit(solution)/shard_map/psum | solution.py:75
  553.5 0.6 broadcast_multiply_fusion
  (33 shorter events, 0.1 us)
Async XLA Ops:
  7.2 398.4 %reduce-scatter.3.cloned.1.call-start = ((), (), s32[]{:S(2)}) async-start(), calls=%async_computation.2 | async-start | bytes 9584640 | tf_op jit(solution)/shard_map/reduce_scatter | solution.py:62
  8.2 17.4 %collective-permute-start = (bf16[2,1,512]{1,2,0:T(8,128)(2,1)S(1)}, bf16[2,1,512]{1,2,0:T(8,128)(2,1)S(1)}, u32[]{:S(2)}, u32[]{:S(2)}) collective-permute-start(bf16[2,1,512]{1,2,0:T(8,128)(2,1)S(1)} %copy.27), channel_id=1, source_target_pairs={{0,1},{1,2},{2,3},{3,4},{4,5},{5,6},{6,7},{7,8},{8,9},{9,10},{10,1... | collective-permute-start | bytes 6152 | tf_op jit(solution)/shard_map/ppermute | solution.py:14
  10.6 15.0 %collective-permute-start.1 = (bf16[2,1,512]{1,2,0:T(8,128)(2,1)S(1)}, bf16[2,1,512]{1,2,0:T(8,128)(2,1)S(1)}, u32[]{:S(2)}, u32[]{:S(2)}) collective-permute-start(bf16[2,1,512]{1,2,0:T(8,128)(2,1)S(1)} %copy.28), channel_id=1, source_target_pairs={{1,0},{2,1},{3,2},{4,3},{5,4},{6,5},{7,6},{8,7},{9,8},{10,9},{11,1... | collective-permute-start | bytes 6152 | tf_op jit(solution)/shard_map/ppermute | solution.py:15
  25.6 0.7 copy-start.14
  26.3 0.7 copy-start.16
  29.4 13.7 %collective-permute-start.2 = (bf16[1,770,512]{2,1,0:T(8,128)(2,1)}, bf16[1,770,512]{2,1,0:T(8,128)(2,1)}, u32[]{:S(2)}, u32[]{:S(2)}) collective-permute-start(bf16[1,770,512]{2,1,0:T(8,128)(2,1)} %copy.30), channel_id=1, source_target_pairs={{64,0},{128,64},{192,128},{65,1},{129,65},{193,129},{66,2},{130,66... | collective-permute-start | bytes 2365448 | tf_op jit(solution)/shard_map/ppermute | solution.py:15
  33.8 14.1 %copy-start.15 = (bf16[2,1,512]{1,2,0:T(8,128)(2,1)S(1)}, bf16[2,1,512]{1,2,0:T(8,128)(2,1)}, u32[]{:S(2)}) copy-start(bf16[2,1,512]{1,2,0:T(8,128)(2,1)} %copy-done.14) | copy-start | bytes 6148
  33.8 11.9 %collective-permute-start.3 = (bf16[1,770,512]{2,1,0:T(8,128)(2,1)}, bf16[1,770,512]{2,1,0:T(8,128)(2,1)}, u32[]{:S(2)}, u32[]{:S(2)}) collective-permute-start(bf16[1,770,512]{2,1,0:T(8,128)(2,1)} %copy.39), channel_id=1, source_target_pairs={{0,64},{64,128},{128,192},{1,65},{65,129},{129,193},{2,66},{66,130... | collective-permute-start | bytes 2365448 | tf_op jit(solution)/shard_map/ppermute | solution.py:14
  40.5 19.2 %copy-start.12 = (bf16[2,768,512]{1,2,0:T(8,128)(2,1)}, bf16[2,768,512]{1,2,0:T(8,128)(2,1)S(1)}, u32[]{:S(2)}) copy-start(bf16[2,768,512]{1,2,0:T(8,128)(2,1)S(1)} %get-tuple-element.12) | copy-start | bytes 4718596
  47.9 4.6 copy-start.17
  52.5 3.0 copy-start.2
  52.5 11.3 %copy-start = (bf16[3,770,512]{1,2,0:T(8,128)(2,1)}, bf16[3,770,512]{1,2,0:T(8,128)(2,1)S(1)}, u32[]{:S(2)}) copy-start(bf16[3,770,512]{1,2,0:T(8,128)(2,1)S(1)} %get-tuple-element.8) | copy-start | bytes 7096324
  55.5 1.4 copy-start.13
  56.9 1.4 copy-start.5
  64.9 3.6 copy-start.4
  68.5 1.4 copy-start.18
  68.5 400.1 %reduce-scatter.5.cloned.1.call-start = ((), (), s32[]{:S(2)}) async-start(), calls=%async_computation.3 | async-start | bytes 184320 | tf_op jit(solution)/shard_map/reduce_scatter | solution.py:70
  73.6 5.4 copy-start.1
  85.9 4.5 copy-start.11
  98.9 2.2 copy-start.10
  101.1 2.2 copy-start.9
  103.3 2.2 copy-start.8
  105.5 2.2 copy-start.6
  107.7 2.2 copy-start.7
  405.5 64.5 %copy-start.3 = (f32[1536,512]{1,0:T(8,128)S(1)}, f32[1536,512]{1,0:T(8,128)}, u32[]{:S(2)}) copy-start(f32[1536,512]{1,0:T(8,128)} %get-tuple-element.16) | copy-start | bytes 9437188
  470.0 83.4 %copy-start.19 = (f32[8,3,3,128]{3,0,2,1:T(8,128)S(1)}, f32[8,3,3,128]{3,0,2,1:T(8,128)}, u32[]{:S(2)}) copy-start(f32[8,3,3,128]{3,0,2,1:T(8,128)} %reduce-scatter.5.cloned.1.call-done) | copy-start | bytes 110596
Sparse Core Ops, SparseCore 0:
  68.6 336.8 reduce-scatter.2
  408.0 60.5 reduce-scatter.4
where the time goes:
time: 562 us; the launch traced here: 561 us
  waiting for transfers between devices  355 us (63%)
  blocking collectives  77 us (14%)
  local copies, waits for them, and re-layouts  41.9 us (7%)
  matrix products  39.5 us (7%)
  starting transfers between devices  17.5 us (3%)
  other arithmetic  15.4 us (3%)
  between operations  15.1 us (3%)
    reduce_scatter x1, waiting for transfers between devices, shards(): lax.psum_scatter(jnp.stack(blocks, axis=1).reshape(channels // lax.axis_s...  290 us
    psum x1, blocking collectives, shards(): grand_total = lax.psum(local_squares, ('lat', 'lon'))  77 us
    reduce_scatter x1, waiting for transfers between devices, shards(): lax.psum_scatter(lon_partial, 'lat', scatter_dimension=3, tiled=True)  57.7 us
    dot_general x9, matrix products, transposed_conv(): lax.dot_general(pieces[position], kernel[lat_pos, lon_pos], (((1,), (1,))...  27.7 us
    slice x9, local copies, waits for them, and re-layouts, shifted_list(): padded[1 - lat_off:1 - lat_off + height, 1 - lon_off:1 - lon_off + breadth]  25.3 us
    ppermute x2, starting transfers between devices, extended(): after = lax.ppermute(first, axis, down)  12.4 us
    dot_general x9, matrix products, shards(): lax.dot_general(shifted, activated, (((0,), (0,)), ((), ())), preferred_e...  11.7 us
  transfers between devices with their start and end apart: 6, of which 5 were waited for; matrix products, arithmetic and copies ran while one was open for 11% of the time, Pallas kernels for 0%

commit v1 on v0

v1 whole, which is shorter than its diff:
```python
import jax
import jax.numpy as jnp
from jax import lax
from jax.experimental import pallas as pl
from jax.experimental.pallas import tpu as pltpu
from jax.sharding import PartitionSpec as P

BF = jnp.bfloat16
F32 = jnp.float32
MESH = pl.DeviceIdType.MESH
B = 768
C = 512
TN = (((0,), (0,)), ((), ()))
NT = (((1,), (1,)), ((), ()))


def sigmoid(v):
    return 1.0 / (1.0 + jnp.exp(-v))


def body(
    pre_hbm, go_hbm, w_hbm, gin_hbm, gk_ref,
    ext, gos, wv, pre_half, pre_own, act, acc, gin,
    px, send_x, recv_x, zx, send_zx, recv_zx, send_yf, recv_yf,
    py, send_y, recv_y, zy, send_z, recv_z, send_xf, recv_xf,
    final, ar_own, ar_core, ar_y, ar_x, ar_z,
    ld_sem, w_sem, out_sem, sib_s, sib_r, rim_s, rim_r, halo_s, halo_r, hrim_s, hrim_r, fwd_s, fwd_r,
    x_s, x_r, zx_s, zx_r, yf_s, yf_r, y_s, y_r, z_s, z_r, xf_s, xf_r, ar_s, ar_r,
):
    lat = lax.axis_index("lat")
    lon = lax.axis_index("lon")
    xlo, core = lat // 2, lat % 2
    z, xh, y = lon // 8, (lon // 4) % 2, lon % 4
    x = xh * 2 + xlo

    sib = (xlo * 2 + 1 - core, lon)
    left, right = lax.rem(lon + 63, 64), lax.rem(lon + 1, 64)

    def y_peer(d):
        to = lax.rem(y + d, 4)
        return to, (lat, (z * 2 + xh) * 4 + to)

    def z_peer(d):
        to = lax.rem(z + d, 8)
        return to, (lat, (to * 2 + xh) * 4 + y)

    def x_peer(d):
        to = lax.rem(x + d, 4)
        return to, (lax.rem(to, 2) * 2 + core, (z * 2 + to // 2) * 4 + y)

    def remote(src, dst, ss, rs, dev):
        return pltpu.make_async_remote_copy(
            src_ref=src, dst_ref=dst, send_sem=ss, recv_sem=rs, device_id=dev, device_id_type=MESH
        )

    bar = pltpu.get_barrier_semaphore()
    peers = [sib]
    for q in range(4):
        for side in (left, right):
            peers.append((q, side))
    peers += [((1 - xlo) * 2 + t, lon) for t in range(2)]
    peers += [y_peer(d)[1] for d in (1, 2, 3)]
    peers += [x_peer(d)[1] for d in (1, 2, 3)]
    peers += [z_peer(d)[1] for d in range(1, 8)]
    for p in peers:
        pl.semaphore_signal(bar, inc=1, device_id=p, device_id_type=MESH)

    own = 1 + 2 * core
    loads = [
        pltpu.make_async_copy(go_hbm, ext.at[pl.ds(own, 2), pl.ds(16, B)], ld_sem.at[0]),
        pltpu.make_async_copy(pre_hbm, pre_own, ld_sem.at[1]),
    ]
    for h in range(2):
        loads.append(
            pltpu.make_async_copy(
                pre_hbm.at[:, :, pl.ds(pl.multiple_of(core * 128, 128) + 256 * h, 128)],
                pre_half.at[pl.ds(2 * core, 2), :, pl.ds(128 * h, 128)],
                ld_sem.at[2 + h],
            )
        )
    for cp in loads:
        cp.start()
    w_loads = []
    for i in range(3):
        for j in range(3):
            cp = pltpu.make_async_copy(w_hbm.at[i, j], wv.at[i, :, pl.ds(512 * j, 512)], w_sem.at[3 * i + j])
            cp.start()
            w_loads.append(cp)

    pl.semaphore_wait(bar, len(peers))

    sib_copies = []
    for m in range(2):
        sib_copies.append(
            remote(go_hbm.at[m], ext.at[own + m, pl.ds(16, B)], sib_s.at[m], sib_r.at[m], sib)
        )
    for h in range(2):
        sib_copies.append(
            remote(
                pre_hbm.at[:, :, pl.ds(pl.multiple_of((1 - core) * 128, 128) + 256 * h, 128)],
                pre_half.at[pl.ds(2 * core, 2), :, pl.ds(128 * h, 128)],
                sib_s.at[2 + h], sib_r.at[2 + h], sib,
            )
        )
    rims = []
    for t in range(2):
        rims.append(
            remote(
                go_hbm.at[:, pl.ds(B - 16, 16)], ext.at[pl.ds(own, 2), pl.ds(0, 16)],
                rim_s.at[0, t], rim_r.at[0, core], (xlo * 2 + t, right),
            )
        )
        rims.append(
            remote(
                go_hbm.at[:, pl.ds(0, 16)], ext.at[pl.ds(own, 2), pl.ds(16 + B, 16)],
                rim_s.at[1, t], rim_r.at[1, core], (xlo * 2 + t, left),
            )
        )
    for cp in rims:
        cp.start()
    for cp in sib_copies:
        cp.start()

    owner = core + xlo == 1
    far = 5 * xlo
    halos = []
    for t in range(2):
        halos.append(
            remote(
                go_hbm.at[core, pl.ds(384 * t, 384)], ext.at[far, pl.ds(16 + 384 * t, 384)],
                halo_s.at[t], halo_r, ((1 - xlo) * 2 + t, lon),
            )
        )
        halos.append(
            remote(
                go_hbm.at[core, pl.ds(B - 16, 16)], ext.at[far, pl.ds(0, 16)],
                hrim_s.at[0, t], hrim_r.at[0], ((1 - xlo) * 2 + t, right),
            )
        )
        halos.append(
            remote(
                go_hbm.at[core, pl.ds(0, 16)], ext.at[far, pl.ds(16 + B, 16)],
                hrim_s.at[1, t], hrim_r.at[1], ((1 - xlo) * 2 + t, left),
            )
        )

    @pl.when(owner)
    def _():
        for cp in halos:
            cp.start()

    def spread(r):
        rows = pl.ds(pl.multiple_of(r * B, B), B)
        gos[rows, 0:512] = ext[r, 17 : 17 + B, :]
        gos[rows, 512:1024] = ext[r, 16 : 16 + B, :]
        gos[rows, 1024:1536] = ext[r, 15 : 15 + B, :]

    def activate(r):
        @pl.loop(0, 3)
        def _(n):
            v = pre_half[r, pl.ds(pl.multiple_of(n * 256, 256), 256), :].astype(F32)
            act[pl.ds(pl.multiple_of(r * B + n * 256, 256), 256), :] = (v * sigmoid(v)).astype(BF)

    zero_row = 5 * xlo
    gos[pl.ds(pl.multiple_of(zero_row * B, B), B), :] = jnp.zeros((B, 1536), BF)

    for cp in loads:
        cp.wait()

    @pl.loop(0, 2)
    def _(m):
        activate(2 * core + m)

    def wait_rims(cc):
        rows = pl.ds(1 + 2 * cc, 2)
        for side, at in ((0, 0), (1, 16 + B)):
            remote(
                ext.at[rows, pl.ds(at, 16)], ext.at[rows, pl.ds(at, 16)],
                rim_s.at[side, 0], rim_r.at[side, cc], sib,
            ).wait_recv()

    wait_rims(core)

    @pl.loop(0, 2)
    def _(m):
        spread(own + m)

    for cp in w_loads:
        cp.wait()

    @pl.loop(0, 6)
    def _(n):
        m, at = n // 3, lax.rem(n, 3) * 256

        def rows(r):
            return pl.ds(pl.multiple_of(r * B + at, 256), 256)

        here = lax.dot_general(gos[rows(own + m), :], wv[1], NT, preferred_element_type=F32)
        there = lax.dot_general(gos[rows(own + 1 - m), :], wv[2 * m], NT, preferred_element_type=F32)
        acc[pl.ds(pl.multiple_of(n * 256, 256), 256), :] = here + there

    other = 1 + 2 * (1 - core)
    for m in range(2):
        remote(
            ext.at[other + m, pl.ds(16, B)], ext.at[other + m, pl.ds(16, B)], sib_s.at[m], sib_r.at[m], sib
        ).wait_recv()
    for h in range(2):
        part = pre_half.at[pl.ds(2 * (1 - core), 2), :, pl.ds(128 * h, 128)]
        remote(part, part, sib_s.at[2 + h], sib_r.at[2 + h], sib).wait_recv()
    wait_rims(1 - core)

    @pl.loop(0, 2)
    def _(m):
        activate(2 * (1 - core) + m)
        spread(other + m)

    def term(j, g0, a0, k):
        return lax.dot_general(
            gos[pl.ds(pl.multiple_of(g0 * B, B), k), pl.ds(pl.multiple_of(j * 512, 512), 512)],
            act[pl.ds(pl.multiple_of(a0 * B, B), k), :],
            TN,
            preferred_element_type=F32,
        )

    def x_copy(j, d):
        to, dev = x_peer(d)
        return remote(send_x.at[j, to], recv_x.at[j, d - 1], x_s.at[j, d - 1], x_r.at[j, d - 1], dev)

    def y_copy(t, d):
        to, dev = y_peer(d)
        return remote(send_y.at[t, to], recv_y.at[t, d - 1], y_s.at[t, d - 1], y_r.at[t, d - 1], dev)

    @pl.loop(0, 3)
    def _(j):
        p = term(j, 1, 0, 4 * B).reshape(8, 2, 32, 256)
        px[j] = p
        for a in range(2):
            for b in range(2):
                send_x[j, 2 * a + b] = p[:, a, :, 128 * b : 128 * b + 128].reshape(256, 128).astype(BF)
        for d in (1, 2, 3):
            x_copy(j, d).start()

    def first_y(t, j, g0, a0, k):
        p = term(j, g0, a0, k).reshape(16, 4, 8, 256)
        py[t] = p
        for to in range(4):
            send_y[t, to] = p[:, to].reshape(128, 256).astype(BF)
        for d in (1, 2, 3):
            y_copy(t, d).start()

    @pl.loop(0, 3)
    def _(j):
        first_y(j, j, 1 + xlo, 1 - xlo, 3 * B)

    near = 5 * (1 - xlo)
    half = ext.at[near, pl.ds(pl.multiple_of(16 + 384 * core, 16), 384)]
    other_half = ext.at[near, pl.ds(pl.multiple_of(16 + 384 * (1 - core), 16), 384)]
    remote(half, half, halo_s.at[0], halo_r, sib).wait_recv()
    forward = remote(half, half, fwd_s, fwd_r, sib)
    forward.start()
    for side, at in ((0, 0), (1, 16 + B)):
        edge = ext.at[near, pl.ds(at, 16)]
        remote(edge, edge, hrim_s.at[side, 0], hrim_r.at[side], sib).wait_recv()
    remote(other_half, other_half, fwd_s, fwd_r, sib).wait_recv()
    spread(near)

    @pl.loop(0, 3)
    def _(j):
        first_y(3 + j, j, 2 * (1 - xlo), 0, 4 * B)

    @pl.loop(0, 6)
    def _(n):
        m, at = n // 3, lax.rem(n, 3) * 256
        src = pl.ds(pl.multiple_of((2 * core + 3 * m) * B + at, 256), 256)
        rest = lax.dot_general(gos[src, :], wv[2 - 2 * m], NT, preferred_element_type=F32)
        grad = acc[pl.ds(pl.multiple_of(n * 256, 256), 256), :] + rest
        cells = pl.ds(pl.multiple_of(at, 256), 256)
        h = pre_own[m, cells, :].astype(F32)
        s = sigmoid(h)
        gin[m, cells, :] = (grad * s * (1.0 + h * (1.0 - s))).astype(BF)

    store = pltpu.make_async_copy(gin, gin_hbm, out_sem)
    store.start()

    def z_copy(g, d):
        to, dev = z_peer(d)
        return remote(send_z.at[g, to], recv_z.at[g, d - 1], z_s.at[g, d - 1], z_r.at[g, d - 1], dev)

    def zx_copy(d):
        to, dev = z_peer(d)
        return remote(send_zx.at[to], recv_zx.at[d - 1], zx_s.at[d - 1], zx_r.at[d - 1], dev)

    def finish_y(g):
        @pl.loop(0, 3)
        def _(j):
            t = 3 * g + j
            total = py[t, :, y].reshape(128, 256)
            for d in (1, 2, 3):
                y_copy(t, d).wait_recv()
                total = total + recv_y[t, d - 1].astype(F32)
            total = total.reshape(8, 16, 256)
            zy[t] = total
            for to in range(8):
                send_z[g, to, j] = total[to].astype(BF)

        for d in range(1, 8):
            z_copy(g, d).start()

    def finish_x():
        @pl.loop(0, 3)
        def _(j):
            total = px[j, :, xh, :, pl.ds(pl.multiple_of(xlo * 128, 128), 128)].reshape(256, 128)
            for d in (1, 2, 3):
                x_copy(j, d).wait_recv()
                total = total + recv_x[j, d - 1].astype(F32)
            total = total.reshape(8, 32, 128)
            zx[j] = total
            for to in range(8):
                send_zx[to, j] = total[to].astype(BF)

        for d in range(1, 8):
            zx_copy(d).start()

    finish_y(0)
    finish_x()
    finish_y(1)

    def finish_z(g, slot):
        for d in range(1, 8):
            z_copy(g, d).wait_recv()

        @pl.loop(0, 3)
        def _(j):
            total = zy[3 * g + j, z]
            for d in range(1, 8):
                total = total + recv_z[g, d - 1, j].astype(F32)
            for a in range(2):
                for b in range(2):
                    send_xf[2 * a + b, slot, j] = total[8 * a : 8 * a + 8, 128 * b : 128 * b + 128]

    def yf_copy(d):
        to, dev = y_peer(d)
        return remote(send_yf.at[to], recv_yf.at[d - 1], yf_s.at[d - 1], yf_r.at[d - 1], dev)

    def xf_copy(d):
        to, dev = x_peer(d)
        return remote(send_xf.at[to], recv_xf.at[d - 1], xf_s.at[d - 1], xf_r.at[d - 1], dev)

    finish_z(0, 1 - xlo)
    for d in range(1, 8):
        zx_copy(d).wait_recv()

    @pl.loop(0, 3)
    def _(j):
        total = zx[j, z]
        for d in range(1, 8):
            total = total + recv_zx[d - 1, j].astype(F32)
        for to in range(4):
            send_yf[to, j] = total[8 * to : 8 * to + 8, :]

    for d in (1, 2, 3):
        yf_copy(d).start()
    finish_z(1, xlo)
    for d in (1, 2, 3):
        xf_copy(d).start()

    for d in (1, 2, 3):
        yf_copy(d).wait_recv()
    final[1] = send_yf[y] + recv_yf[0] + recv_yf[1] + recv_yf[2]
    for d in (1, 2, 3):
        xf_copy(d).wait_recv()
    for gi in range(2):
        final[2 * gi] = send_xf[x, gi] + recv_xf[0, gi] + recv_xf[1, gi] + recv_xf[2, gi]

    all_terms = final[...].reshape(9, 8, 128)
    total = jnp.sum(all_terms * all_terms, axis=0)
    ar_own[0] = total
    cp = remote(ar_own.at[0], ar_core, ar_s.at[0], ar_r.at[0], sib)
    cp.start()
    sums = [cp]
    cp.wait_recv()
    total = total + ar_core[...]
    at = 1
    for stage, (peer, count, slots) in enumerate(((y_peer, 3, ar_y), (x_peer, 3, ar_x), (z_peer, 7, ar_z))):
        ar_own[1 + stage] = total
        copies = []
        for d in range(1, count + 1):
            cp = remote(ar_own.at[1 + stage], slots.at[d - 1], ar_s.at[at], ar_r.at[at], peer(d)[1])
            at = at + 1
            cp.start()
            copies.append(cp)
        for cp in copies:
            cp.wait_recv()
        for d in range(count):
            total = total + slots[d]
        sums += copies
    grand = jnp.sum(total)
    factor = jnp.float32(3.0 * C) * lax.rsqrt(jnp.full((8, 128), grand, F32) + 1e-06)
    for i in range(3):
        for j in range(3):
            gk_ref[:, i, j, :] = final[i, j] * factor

    for cp in rims + sib_copies:
        cp.wait_send()

    @pl.when(owner)
    def _():
        for cp in halos:
            cp.wait_send()

    forward.wait_send()
    for d in (1, 2, 3):
        for j in range(3):
            x_copy(j, d).wait_send()
        for t in range(6):
            y_copy(t, d).wait_send()
        yf_copy(d).wait_send()
        xf_copy(d).wait_send()
    for d in range(1, 8):
        for g in range(2):
            z_copy(g, d).wait_send()
        zx_copy(d).wait_send()
    for cp in sums:
        cp.wait_send()
    store.wait()


def shards(pre_act, grad_out, kernel):
    vmem = pltpu.VMEM
    dma = pltpu.SemaphoreType.DMA
    scratch = [
        vmem((6, B + 32, C), BF),
        vmem((6 * B, 3 * C), BF),
        vmem((3, C, 3 * C), BF),
        vmem((4, B, 256), BF),
        vmem((2, B, C), BF),
        vmem((4 * B, 256), BF),
        vmem((2 * B, C), F32),
        vmem((2, B, C), BF),
        vmem((3, 8, 2, 32, 256), F32),
        vmem((3, 4, 256, 128), BF),
        vmem((3, 3, 256, 128), BF),
        vmem((3, 8, 32, 128), F32),
        vmem((8, 3, 32, 128), BF),
        vmem((7, 3, 32, 128), BF),
        vmem((4, 3, 8, 128), F32),
        vmem((3, 3, 8, 128), F32),
        vmem((6, 16, 4, 8, 256), F32),
        vmem((6, 4, 128, 256), BF),
        vmem((6, 3, 128, 256), BF),
        vmem((6, 8, 16, 256), F32),
        vmem((2, 8, 3, 16, 256), BF),
        vmem((2, 7, 3, 16, 256), BF),
        vmem((4, 2, 3, 8, 128), F32),
        vmem((3, 2, 3, 8, 128), F32),
        vmem((3, 3, 8, 128), F32),
        vmem((4, 8, 128), F32),
        vmem((8, 128), F32),
        vmem((3, 8, 128), F32),
        vmem((3, 8, 128), F32),
        vmem((7, 8, 128), F32),
        dma((4,)), dma((9,)), dma, dma((4,)), dma((4,)), dma((2, 2)), dma((2, 2)),
        dma((2,)), dma, dma((2, 2)), dma((2,)), dma, dma,
        dma((3, 3)), dma((3, 3)), dma((7,)), dma((7,)), dma((3,)), dma((3,)),
        dma((6, 3)), dma((6, 3)), dma((2, 7)), dma((2, 7)), dma((3,)), dma((3,)), dma((14,)), dma((14,)),
    ]
    return pl.pallas_call(
        body,
        out_shape=(
            jax.ShapeDtypeStruct((2, B, C), BF),
            jax.ShapeDtypeStruct((8, 3, 3, 128), F32),
        ),
        in_specs=[pl.BlockSpec(memory_space=pl.ANY)] * 3,
        out_specs=(pl.BlockSpec(memory_space=pl.ANY), pl.BlockSpec(memory_space=pltpu.VMEM)),
        scratch_shapes=scratch,
        compiler_params=pltpu.CompilerParams(
            collective_id=0, has_side_effects=True, vmem_limit_bytes=58 * 2**20
        ),
        cost_estimate=pl.CostEstimate(flops=14_500_000_000, bytes_accessed=12_000_000, transcendentals=1_600_000),
        name="conv_backward",
    )(pre_act, grad_out, kernel)


def solution(mesh):
    in_specs = (P("lat", "lon", None), P("lat", "lon", None), P())
    out_specs = (P("lat", "lon", None), P("lon", None, None, "lat"))
    return jax.shard_map(shards, mesh=mesh, in_specs=in_specs, out_specs=out_specs, check_vma=False)
```

time: 562 us -> 76.3 us (0.14)
  waiting for transfers between devices: 355 us -> 0 us
  blocking collectives: 77 us -> 0 us
  Pallas kernels: 0 us -> 71.5 us
  matrix products: 39.5 us -> 0 us
  local copies, waits for them, and re-layouts: 41.9 us -> 4.07 us
  starting transfers between devices: 17.5 us -> 0 us
  other arithmetic: 15.4 us -> 0 us
  between operations: 15.1 us -> 0.64 us
    reduce_scatter x2 -> x0, waiting for transfers between devices: 348 us -> none  [the longest x1 290 us: shards(): lax.psum_scatter(jnp.stack(blocks, axis=1).reshape(channels // lax.axis_s...]
    psum x1 -> x0, blocking collectives: 77 us -> none  [shards(): grand_total = lax.psum(local_squares, ('lat', 'lon'))]
    pallas_call x0 -> x1, Pallas kernels: none -> 71.5 us  [shards(): pl.pallas_call(body, out_shape=(jax.ShapeDtypeStruct((2, B, C), BF), jax....]
    dot_general x18 -> x0, matrix products: 39.5 us -> none  [the longest x9 27.7 us: transposed_conv(): lax.dot_general(pieces[position], kernel[lat_pos, lon_pos], (((1,), (1,))...]
    slice x15 -> x0, local copies, waits for them, and re-layouts: 29 us -> none  [the longest x9 25.3 us: shifted_list(): padded[1 - lat_off:1 - lat_off + height, 1 - lon_off:1 - lon_off + breadth]]
    ppermute x4 -> x0, starting transfers between devices: 17.2 us -> none  [the longest x2 12.4 us: extended(): after = lax.ppermute(first, axis, down)]
    concatenate x3 -> x0, other arithmetic: 9.73 us -> none  [extended(): shard = jnp.concatenate([before, shard, after], axis=dim)]
    ppermute x4 -> x0, waiting for transfers between devices: 6.98 us -> none  [the longest x2 4.34 us: extended(): before = lax.ppermute(last, axis, up)]
  transfers between devices with their start and end apart: 6 -> 0, of which waited for: 5 -> 0; matrix products, arithmetic and copies ran while one was open for 11% -> 0% of each run, Pallas kernels for 0% -> 0%
where the time goes in v1:
time: 76.3 us; the launch traced here: 76.2 us
  Pallas kernels  71.5 us (94%)
  local copies, waits for them, and re-layouts  4.07 us (5%)
    pallas_call x1, Pallas kernels, shards(): pl.pallas_call(body, out_shape=(jax.ShapeDtypeStruct((2, B, C), BF), jax....  71.5 us
    unnamed x1, local copies, waits for them, and re-layouts  2.65 us

profile of v1, /device:TPU:1, one launch (start us, length us, event | category | flops | bytes accessed | tf_op | source)
XLA Modules:
  0.0 76.2 jit_solution(18279740005611362009)
XLA Ops:
  0.6 71.5 %conv_backward.1 = (bf16[2,768,512]{2,1,0:T(8,128)(2,1)}, f32[8,3,3,128]{3,2,1,0:T(4,128)}) custom-call(bf16[2,768,512]{2,1,0:T(8,128)(2,1)} %pre_hbm.1, bf16[2,768,512]{2,1,0:T(8,128)(2,1)} %go_hbm.1, bf16[3,3,512,512]{3,2,1,0:T(8,128)(2,1)} %w_hbm.1), custom_call_target="tpu_custom_call" | custom-call | flops 14499999744 | bytes 12000000 | tf_op jit(solution)/shard_map/conv_backward/pallas_call | solution.py:467
  72.1 1.4 %copy.5 = f32[8,3,3,128]{3,0,2,1:T(8,128)} copy(f32[8,3,3,128]{3,2,1,0:T(4,128)} %get-tuple-element.3) | data formatting | bytes 73728 | tf_op jit(solution)/shard_map/conv_backward/pallas_call | solution.py:467
  73.5 2.7 %copy.7 = bf16[2,768,512]{2,1,0:T(8,128)(2,1)} copy(bf16[2,768,512]{2,1,0:T(8,128)(2,1)} %get-tuple-element.6) | data formatting | bytes 3145728

commit v2 on v1

--- a/solution.py
+++ b/solution.py
@@ -21,11 +21,13 @@
 def body(
     pre_hbm, go_hbm, w_hbm, gin_hbm, gk_ref,
     ext, gos, wv, pre_half, pre_own, act, acc, gin,
-    px, send_x, recv_x, zx, send_zx, recv_zx, send_yf, recv_yf,
-    py, send_y, recv_y, zy, send_z, recv_z, send_xf, recv_xf,
+    px, send_x, recv_x, mx_own, send_my, recv_my,
+    py, send_y, recv_y, my_own, send_mx, recv_mx,
+    pz, send_z, recv_z, mz_own, send_mz, recv_mz,
+    send_zf, recv_zf, send_xf, recv_xf,
     final, ar_own, ar_core, ar_y, ar_x, ar_z,
     ld_sem, w_sem, out_sem, sib_s, sib_r, rim_s, rim_r, halo_s, halo_r, hrim_s, hrim_r, fwd_s, fwd_r,
-    x_s, x_r, zx_s, zx_r, yf_s, yf_r, y_s, y_r, z_s, z_r, xf_s, xf_r, ar_s, ar_r,
+    x_s, x_r, my_s, my_r, y_s, y_r, mx_s, mx_r, z_s, z_r, mz_s, mz_r, zf_s, zf_r, xf_s, xf_r, ar_s, ar_r,
 ):
     lat = lax.axis_index("lat")
     lon = lax.axis_index("lon")
@@ -185,11 +187,7 @@
     def _(m):
         spread(own + m)
 
-    for cp in w_loads:
-        cp.wait()
-
-    @pl.loop(0, 6)
-    def _(n):
+    def own_share(n):
         m, at = n // 3, lax.rem(n, 3) * 256
 
         def rows(r):
@@ -230,8 +228,11 @@
         to, dev = y_peer(d)
         return remote(send_y.at[t, to], recv_y.at[t, d - 1], y_s.at[t, d - 1], y_r.at[t, d - 1], dev)
 
-    @pl.loop(0, 3)
-    def _(j):
+    def z_copy(g, d):
+        to, dev = z_peer(d)
+        return remote(send_z.at[g, to], recv_z.at[g, d - 1], z_s.at[g, d - 1], z_r.at[g, d - 1], dev)
+
+    def first_x(j):
         p = term(j, 1, 0, 4 * B).reshape(8, 2, 32, 256)
         px[j] = p
         for a in range(2):
@@ -248,9 +249,19 @@
         for d in (1, 2, 3):
             y_copy(t, d).start()
 
-    @pl.loop(0, 3)
+    def first_z(g, j, g0, a0, k):
+        p = term(j, g0, a0, k).reshape(8, 64, 256)
+        pz[g] = p
+        send_z[g] = p.astype(BF)
+        for d in range(1, 8):
+            z_copy(g, d).start()
+
+    first_z(0, 2, 1 + xlo, 1 - xlo, 3 * B)
+
+    @pl.loop(0, 2)
     def _(j):
         first_y(j, j, 1 + xlo, 1 - xlo, 3 * B)
+        first_x(j)
 
     near = 5 * (1 - xlo)
     half = ext.at[near, pl.ds(pl.multiple_of(16 + 384 * core, 16), 384)]
@@ -258,119 +269,180 @@
     remote(half, half, halo_s.at[0], halo_r, sib).wait_recv()
     forward = remote(half, half, fwd_s, fwd_r, sib)
     forward.start()
+    first_x(2)
+
     for side, at in ((0, 0), (1, 16 + B)):
         edge = ext.at[near, pl.ds(at, 16)]
         remote(edge, edge, hrim_s.at[side, 0], hrim_r.at[side], sib).wait_recv()
     remote(other_half, other_half, fwd_s, fwd_r, sib).wait_recv()
     spread(near)
 
+    first_z(1, 2, 2 * (1 - xlo), 0, 4 * B)
+
+    @pl.loop(0, 2)
+    def _(j):
+        first_y(2 + j, j, 2 * (1 - xlo), 0, 4 * B)
+
+    for cp in w_loads:
+        cp.wait()
+
     @pl.loop(0, 3)
-    def _(j):
-        first_y(3 + j, j, 2 * (1 - xlo), 0, 4 * B)
-
-    @pl.loop(0, 6)
     def _(n):
+        own_share(n)
+
+    def rest(n):
         m, at = n // 3, lax.rem(n, 3) * 256
         src = pl.ds(pl.multiple_of((2 * core + 3 * m) * B + at, 256), 256)
-        rest = lax.dot_general(gos[src, :], wv[2 - 2 * m], NT, preferred_element_type=F32)
-        grad = acc[pl.ds(pl.multiple_of(n * 256, 256), 256), :] + rest
+        other_row = lax.dot_general(gos[src, :], wv[2 - 2 * m], NT, preferred_element_type=F32)
+        grad = acc[pl.ds(pl.multiple_of(n * 256, 256), 256), :] + other_row
         cells = pl.ds(pl.multiple_of(at, 256), 256)
         h = pre_own[m, cells, :].astype(F32)
         s = sigmoid(h)
         gin[m, cells, :] = (grad * s * (1.0 + h * (1.0 - s))).astype(BF)
 
     store = pltpu.make_async_copy(gin, gin_hbm, out_sem)
-    store.start()
-
-    def z_copy(g, d):
-        to, dev = z_peer(d)
-        return remote(send_z.at[g, to], recv_z.at[g, d - 1], z_s.at[g, d - 1], z_r.at[g, d - 1], dev)
-
-    def zx_copy(d):
-        to, dev = z_peer(d)
-        return remote(send_zx.at[to], recv_zx.at[d - 1], zx_s.at[d - 1], zx_r.at[d - 1], dev)
-
-    def finish_y(g):
+
+    def my_copy(d):
+        to, dev = y_peer(d)
+        return remote(send_my.at[to], recv_my.at[d - 1], my_s.at[d - 1], my_r.at[d - 1], dev)
+
+    def mx_copy(gi, d):
+        to, dev = x_peer(d)
+        return remote(send_mx.at[to, gi], recv_mx.at[d - 1, gi], mx_s.at[gi, d - 1], mx_r.at[gi, d - 1], dev)
+
+    def mz_copy(g, d):
+        to, dev = y_peer(d)
+        return remote(send_mz.at[g, to], recv_mz.at[g, d - 1], mz_s.at[g, d - 1], mz_r.at[g, d - 1], dev)
+
+    my_lanes = pl.ds(pl.multiple_of(xlo * 128, 128), 128)
+
+    def finish_x():
         @pl.loop(0, 3)
         def _(j):
-            t = 3 * g + j
+            total = px[j, :, xh, :, my_lanes].reshape(256, 128)
+            for d in (1, 2, 3):
+                x_copy(j, d).wait_recv()
+                total = total + recv_x[j, d - 1].astype(F32)
+            total = total.reshape(8, 4, 8, 128)
+            mx_own[j] = total
+            for to in range(4):
+                send_my[to, j] = total[:, to].reshape(64, 128).astype(BF)
+
+        for d in (1, 2, 3):
+            my_copy(d).start()
+
+    def finish_y(g, gi):
+        @pl.loop(0, 2)
+        def _(j):
+            t = 2 * g + j
             total = py[t, :, y].reshape(128, 256)
             for d in (1, 2, 3):
                 y_copy(t, d).wait_recv()
                 total = total + recv_y[t, d - 1].astype(F32)
-            total = total.reshape(8, 16, 256)
-            zy[t] = total
-            for to in range(8):
-                send_z[g, to, j] = total[to].astype(BF)
-
-        for d in range(1, 8):
-            z_copy(g, d).start()
-
-    def finish_x():
-        @pl.loop(0, 3)
-        def _(j):
-            total = px[j, :, xh, :, pl.ds(pl.multiple_of(xlo * 128, 128), 128)].reshape(256, 128)
-            for d in (1, 2, 3):
-                x_copy(j, d).wait_recv()
-                total = total + recv_x[j, d - 1].astype(F32)
-            total = total.reshape(8, 32, 128)
-            zx[j] = total
-            for to in range(8):
-                send_zx[to, j] = total[to].astype(BF)
-
-        for d in range(1, 8):
-            zx_copy(d).start()
-
-    finish_y(0)
-    finish_x()
-    finish_y(1)
-
-    def finish_z(g, slot):
+            total = total.reshape(8, 2, 8, 256)
+            my_own[gi, j] = total
+            for a in range(2):
+                for b in range(2):
+                    part = total[:, a, :, 128 * b : 128 * b + 128]
+                    send_mx[2 * a + b, gi, j] = part.reshape(64, 128).astype(BF)
+
+        for d in (1, 2, 3):
+            mx_copy(gi, d).start()
+
+    def finish_z(g):
+        total = pz[g, z]
         for d in range(1, 8):
             z_copy(g, d).wait_recv()
-
-        @pl.loop(0, 3)
-        def _(j):
-            total = zy[3 * g + j, z]
-            for d in range(1, 8):
-                total = total + recv_z[g, d - 1, j].astype(F32)
-            for a in range(2):
-                for b in range(2):
-                    send_xf[2 * a + b, slot, j] = total[8 * a : 8 * a + 8, 128 * b : 128 * b + 128]
-
-    def yf_copy(d):
-        to, dev = y_peer(d)
-        return remote(send_yf.at[to], recv_yf.at[d - 1], yf_s.at[d - 1], yf_r.at[d - 1], dev)
+            total = total + recv_z[g, d - 1].astype(F32)
+        total = total.reshape(2, 4, 8, 256)
+        mz_own[g] = total
+        for to in range(4):
+            send_mz[g, to] = total[:, to].reshape(16, 256).astype(BF)
+        for d in (1, 2, 3):
+            mz_copy(g, d).start()
+
+    finish_x()
+    finish_z(0)
+    finish_y(0, 1 - xlo)
+
+    @pl.loop(3, 6)
+    def _(n):
+        own_share(n)
+
+    def zf_copy(part, d):
+        to, dev = z_peer(d)
+        which = (pl.ds(0, 3), pl.ds(3, 4))[part]
+        return remote(
+            send_zf.at[to, which], recv_zf.at[d - 1, which], zf_s.at[part, d - 1], zf_r.at[part, d - 1], dev
+        )
 
     def xf_copy(d):
         to, dev = x_peer(d)
         return remote(send_xf.at[to], recv_xf.at[d - 1], xf_s.at[d - 1], xf_r.at[d - 1], dev)
 
-    finish_z(0, 1 - xlo)
-    for d in range(1, 8):
-        zx_copy(d).wait_recv()
+    for d in (1, 2, 3):
+        my_copy(d).wait_recv()
 
     @pl.loop(0, 3)
     def _(j):
-        total = zx[j, z]
-        for d in range(1, 8):
-            total = total + recv_zx[d - 1, j].astype(F32)
-        for to in range(4):
-            send_yf[to, j] = total[8 * to : 8 * to + 8, :]
-
-    for d in (1, 2, 3):
-        yf_copy(d).start()
-    finish_z(1, xlo)
+        total = mx_own[j, :, y].reshape(64, 128)
+        for d in range(3):
+            total = total + recv_my[d, j].astype(F32)
+        send_zf[:, j] = total.reshape(8, 8, 128)
+
+    for d in range(1, 8):
+        zf_copy(0, d).start()
+
+    finish_z(1)
+    finish_y(1, xlo)
+
+    @pl.loop(0, 3)
+    def _(n):
+        rest(n)
+
+    for g in range(2):
+        slot = (1 - xlo, xlo)[g]
+        total = mz_own[g, :, y].reshape(16, 256)
+        for d in (1, 2, 3):
+            mz_copy(g, d).wait_recv()
+            total = total + recv_mz[g, d - 1].astype(F32)
+        for a in range(2):
+            for b in range(2):
+                send_xf[2 * a + b, slot] = total[8 * a : 8 * a + 8, 128 * b : 128 * b + 128]
     for d in (1, 2, 3):
         xf_copy(d).start()
 
-    for d in (1, 2, 3):
-        yf_copy(d).wait_recv()
-    final[1] = send_yf[y] + recv_yf[0] + recv_yf[1] + recv_yf[2]
+    for gi in range(2):
+        for d in (1, 2, 3):
+            mx_copy(gi, d).wait_recv()
+        for j in range(2):
+            total = my_own[gi, j, :, xh, :, my_lanes].reshape(64, 128)
+            for d in range(3):
+                total = total + recv_mx[d, gi, j].astype(F32)
+            send_zf[:, 3 + 2 * gi + j] = total.reshape(8, 8, 128)
+    for d in range(1, 8):
+        zf_copy(1, d).start()
+
+    @pl.loop(3, 6)
+    def _(n):
+        rest(n)
+
+    store.start()
+
     for d in (1, 2, 3):
         xf_copy(d).wait_recv()
     for gi in range(2):
-        final[2 * gi] = send_xf[x, gi] + recv_xf[0, gi] + recv_xf[1, gi] + recv_xf[2, gi]
+        final[2 * gi, 2] = send_xf[x, gi] + recv_xf[0, gi] + recv_xf[1, gi] + recv_xf[2, gi]
+    for part in range(2):
+        total = send_zf[z, pl.ds(3 * part, 3 + part)]
+        for d in range(1, 8):
+            zf_copy(part, d).wait_recv()
+            total = total + recv_zf[d - 1, pl.ds(3 * part, 3 + part)]
+        if part == 0:
+            final[1] = total
+        else:
+            for gi in range(2):
+                final[2 * gi, 0:2] = total[2 * gi : 2 * gi + 2]
 
     all_terms = final[...].reshape(9, 8, 128)
     total = jnp.sum(all_terms * all_terms, axis=0)
@@ -398,7 +470,7 @@
     factor = jnp.float32(3.0 * C) * lax.rsqrt(jnp.full((8, 128), grand, F32) + 1e-06)
     for i in range(3):
         for j in range(3):
-            gk_ref[:, i, j, :] = final[i, j] * factor
+            gk_ref[i, j] = final[i, j] * factor
 
     for cp in rims + sib_copies:
         cp.wait_send()
@@ -412,14 +484,17 @@
     for d in (1, 2, 3):
         for j in range(3):
             x_copy(j, d).wait_send()
-        for t in range(6):
+        for t in range(4):
             y_copy(t, d).wait_send()
-        yf_copy(d).wait_send()
+        for g in range(2):
+            mx_copy(g, d).wait_send()
+            mz_copy(g, d).wait_send()
+        my_copy(d).wait_send()
         xf_copy(d).wait_send()
     for d in range(1, 8):
         for g in range(2):
             z_copy(g, d).wait_send()
-        zx_copy(d).wait_send()
+            zf_copy(g, d).wait_send()
     for cp in sums:
         cp.wait_send()
     store.wait()
@@ -440,19 +515,25 @@
         vmem((3, 8, 2, 32, 256), F32),
         vmem((3, 4, 256, 128), BF),
         vmem((3, 3, 256, 128), BF),
-        vmem((3, 8, 32, 128), F32),
-        vmem((8, 3, 32, 128), BF),
-        vmem((7, 3, 32, 128), BF),
-        vmem((4, 3, 8, 128), F32),
-        vmem((3, 3, 8, 128), F32),
-        vmem((6, 16, 4, 8, 256), F32),
-        vmem((6, 4, 128, 256), BF),
-        vmem((6, 3, 128, 256), BF),
-        vmem((6, 8, 16, 256), F32),
-        vmem((2, 8, 3, 16, 256), BF),
-        vmem((2, 7, 3, 16, 256), BF),
-        vmem((4, 2, 3, 8, 128), F32),
-        vmem((3, 2, 3, 8, 128), F32),
+        vmem((3, 8, 4, 8, 128), F32),
+        vmem((4, 3, 64, 128), BF),
+        vmem((3, 3, 64, 128), BF),
+        vmem((4, 16, 4, 8, 256), F32),
+        vmem((4, 4, 128, 256), BF),
+        vmem((4, 3, 128, 256), BF),
+        vmem((2, 2, 8, 2, 8, 256), F32),
+        vmem((4, 2, 2, 64, 128), BF),
+        vmem((3, 2, 2, 64, 128), BF),
+        vmem((2, 8, 64, 256), F32),
+        vmem((2, 8, 64, 256), BF),
+        vmem((2, 7, 64, 256), BF),
+        vmem((2, 2, 4, 8, 256), F32),
+        vmem((2, 4, 16, 256), BF),
+        vmem((2, 3, 16, 256), BF),
+        vmem((8, 7, 8, 128), F32),
+        vmem((7, 7, 8, 128), F32),
+        vmem((4, 2, 8, 128), F32),
+        vmem((3, 2, 8, 128), F32),
         vmem((3, 3, 8, 128), F32),
         vmem((4, 8, 128), F32),
         vmem((8, 128), F32),
@@ -461,24 +542,27 @@
         vmem((7, 8, 128), F32),
         dma((4,)), dma((9,)), dma, dma((4,)), dma((4,)), dma((2, 2)), dma((2, 2)),
         dma((2,)), dma, dma((2, 2)), dma((2,)), dma, dma,
-        dma((3, 3)), dma((3, 3)), dma((7,)), dma((7,)), dma((3,)), dma((3,)),
-        dma((6, 3)), dma((6, 3)), dma((2, 7)), dma((2, 7)), dma((3,)), dma((3,)), dma((14,)), dma((14,)),
+        dma((3, 3)), dma((3, 3)), dma((3,)), dma((3,)),
+        dma((4, 3)), dma((4, 3)), dma((2, 3)), dma((2, 3)),
+        dma((2, 7)), dma((2, 7)), dma((2, 3)), dma((2, 3)),
+        dma((2, 7)), dma((2, 7)), dma((3,)), dma((3,)), dma((14,)), dma((14,)),
     ]
-    return pl.pallas_call(
+    grad_in, grad_kernel = pl.pallas_call(
         body,
         out_shape=(
             jax.ShapeDtypeStruct((2, B, C), BF),
-            jax.ShapeDtypeStruct((8, 3, 3, 128), F32),
+            jax.ShapeDtypeStruct((3, 3, 8, 128), F32),
         ),
         in_specs=[pl.BlockSpec(memory_space=pl.ANY)] * 3,
         out_specs=(pl.BlockSpec(memory_space=pl.ANY), pl.BlockSpec(memory_space=pltpu.VMEM)),
         scratch_shapes=scratch,
         compiler_params=pltpu.CompilerParams(
-            collective_id=0, has_side_effects=True, vmem_limit_bytes=58 * 2**20
+            collective_id=0, has_side_effects=True, vmem_limit_bytes=52 * 2**20
         ),
         cost_estimate=pl.CostEstimate(flops=14_500_000_000, bytes_accessed=12_000_000, transcendentals=1_600_000),
         name="conv_backward",
     )(pre_act, grad_out, kernel)
+    return grad_in, jnp.transpose(grad_kernel, (2, 0, 1, 3))
 
 
 def solution(mesh):

time: 76.3 us -> 65.8 us (0.86)
  Pallas kernels: 71.5 us -> 63.3 us
  local copies, waits for them, and re-layouts: 4.07 us -> 1.76 us
    pallas_call x1, Pallas kernels: 71.5 us -> 63.3 us  [shards(): pl.pallas_call(body, out_shape=(jax.ShapeDtypeStruct((2, B, C), BF), jax....]
    pallas_call x1 -> x0, local copies, waits for them, and re-layouts: 1.42 us -> none  [shards(): pl.pallas_call(body, out_shape=(jax.ShapeDtypeStruct((2, B, C), BF), jax....]
    unnamed x1 -> x2, local copies, waits for them, and re-layouts: 2.65 us -> 1.76 us
where the time goes in v2:
time: 65.8 us; the launch traced here: 65.7 us
  Pallas kernels  63.3 us (96%)
  local copies, waits for them, and re-layouts  1.76 us (3%)
    pallas_call x1, Pallas kernels, shards(): pl.pallas_call(body, out_shape=(jax.ShapeDtypeStruct((2, B, C), BF), jax....  63.3 us
    unnamed x2, local copies, waits for them, and re-layouts  1.76 us

profile of v2, /device:TPU:1, one launch (start us, length us, event | category | flops | bytes accessed | tf_op | source)
XLA Modules:
  0.0 65.7 jit_solution(8443280475350768303)
XLA Ops:
  0.6 63.3 %conv_backward.1 = (bf16[2,768,512]{2,1,0:T(8,128)(2,1)S(1)}, f32[3,3,8,128]{3,2,1,0:T(8,128)S(1)}) custom-call(bf16[2,768,512]{2,1,0:T(8,128)(2,1)} %pre_hbm.1, bf16[2,768,512]{2,1,0:T(8,128)(2,1)} %go_hbm.1, bf16[3,3,512,512]{3,2,1,0:T(8,128)(2,1)} %w_hbm.1), custom_call_target="tpu_custom_call" | custom-call | flops 14499999744 | bytes 12000000 | tf_op jit(solution)/shard_map/conv_backward/pallas_call | solution.py:550
  63.9 1.1 %copy.7 = bf16[2,768,512]{2,1,0:T(8,128)(2,1)} copy(bf16[2,768,512]{2,1,0:T(8,128)(2,1)S(1)} %get-tuple-element.8) | data formatting | bytes 3145728
  65.1 0.6 copy.8

commit v3 on v2

--- a/solution.py
+++ b/solution.py
@@ -25,7 +25,7 @@
     py, send_y, recv_y, my_own, send_mx, recv_mx,
     pz, send_z, recv_z, mz_own, send_mz, recv_mz,
     send_zf, recv_zf, send_xf, recv_xf,
-    final, ar_own, ar_core, ar_y, ar_x, ar_z,
+    final, ar_own, ar_core, ar_xy, ar_z,
     ld_sem, w_sem, out_sem, sib_s, sib_r, rim_s, rim_r, halo_s, halo_r, hrim_s, hrim_r, fwd_s, fwd_r,
     x_s, x_r, my_s, my_r, y_s, y_r, mx_s, mx_r, z_s, z_r, mz_s, mz_r, zf_s, zf_r, xf_s, xf_r, ar_s, ar_r,
 ):
@@ -50,20 +50,23 @@
         to = lax.rem(x + d, 4)
         return to, (lax.rem(to, 2) * 2 + core, (z * 2 + to // 2) * 4 + y)
 
+    def plane_peer(d):
+        tx, ty = lax.rem(x + d % 4, 4), lax.rem(y + d // 4, 4)
+        return tx * 4 + ty, (lax.rem(tx, 2) * 2 + core, (z * 2 + tx // 2) * 4 + ty)
+
     def remote(src, dst, ss, rs, dev):
         return pltpu.make_async_remote_copy(
             src_ref=src, dst_ref=dst, send_sem=ss, recv_sem=rs, device_id=dev, device_id_type=MESH
         )
 
     bar = pltpu.get_barrier_semaphore()
-    peers = [sib]
-    for q in range(4):
-        for side in (left, right):
+    peers = [z_peer(d)[1] for d in (4, 3, 5, 2, 6, 1, 7)]
+    for side in (left, right):
+        for q in range(4):
             peers.append((q, side))
+    peers += [plane_peer(d)[1] for d in range(1, 16)]
     peers += [((1 - xlo) * 2 + t, lon) for t in range(2)]
-    peers += [y_peer(d)[1] for d in (1, 2, 3)]
-    peers += [x_peer(d)[1] for d in (1, 2, 3)]
-    peers += [z_peer(d)[1] for d in range(1, 8)]
+    peers.append(sib)
     for p in peers:
         pl.semaphore_signal(bar, inc=1, device_id=p, device_id_type=MESH)
 
@@ -82,13 +85,6 @@
         )
     for cp in loads:
         cp.start()
-    w_loads = []
-    for i in range(3):
-        for j in range(3):
-            cp = pltpu.make_async_copy(w_hbm.at[i, j], wv.at[i, :, pl.ds(512 * j, 512)], w_sem.at[3 * i + j])
-            cp.start()
-            w_loads.append(cp)
-
     pl.semaphore_wait(bar, len(peers))
 
     sib_copies = []
@@ -151,10 +147,19 @@
         for cp in halos:
             cp.start()
 
-    def spread(r):
+    w_loads = []
+    for i in range(3):
+        for j in range(3):
+            cp = pltpu.make_async_copy(w_hbm.at[i, j], wv.at[i, :, pl.ds(512 * j, 512)], w_sem.at[3 * i + j])
+            cp.start()
+            w_loads.append(cp)
+
+    def centre(r):
+        gos[pl.ds(pl.multiple_of(r * B, B), B), 512:1024] = ext[r, 16 : 16 + B, :]
+
+    def sides(r):
         rows = pl.ds(pl.multiple_of(r * B, B), B)
         gos[rows, 0:512] = ext[r, 17 : 17 + B, :]
-        gos[rows, 512:1024] = ext[r, 16 : 16 + B, :]
         gos[rows, 1024:1536] = ext[r, 15 : 15 + B, :]
 
     def activate(r):
@@ -172,6 +177,7 @@
     @pl.loop(0, 2)
     def _(m):
         activate(2 * core + m)
+        centre(own + m)
 
     def wait_rims(cc):
         rows = pl.ds(1 + 2 * cc, 2)
@@ -181,21 +187,35 @@
                 rim_s.at[side, 0], rim_r.at[side, cc], sib,
             ).wait_recv()
 
+    def term(j, g0, a0, k):
+        return lax.dot_general(
+            gos[pl.ds(pl.multiple_of(g0 * B, B), k), pl.ds(pl.multiple_of(j * 512, 512), 512)],
+            act[pl.ds(pl.multiple_of(a0 * B, B), k), :],
+            TN,
+            preferred_element_type=F32,
+        )
+
+    def own_rows(j):
+        px[j] = term(j, own, 2 * core, 2 * B).reshape(8, 2, 32, 256)
+
+    def own_pair(j):
+        return term(j, own + xlo, 2 * core + 1 - xlo, B)
+
+    own_rows(1)
+    py[1] = own_pair(1).reshape(16, 4, 8, 256)
+
     wait_rims(core)
 
     @pl.loop(0, 2)
     def _(m):
-        spread(own + m)
-
-    def own_share(n):
-        m, at = n // 3, lax.rem(n, 3) * 256
-
-        def rows(r):
-            return pl.ds(pl.multiple_of(r * B + at, 256), 256)
-
-        here = lax.dot_general(gos[rows(own + m), :], wv[1], NT, preferred_element_type=F32)
-        there = lax.dot_general(gos[rows(own + 1 - m), :], wv[2 * m], NT, preferred_element_type=F32)
-        acc[pl.ds(pl.multiple_of(n * 256, 256), 256), :] = here + there
+        sides(own + m)
+
+    py[0] = own_pair(0).reshape(16, 4, 8, 256)
+    pz[0] = own_pair(2).reshape(8, 64, 256)
+
+    @pl.loop(0, 2)
+    def _(n):
+        own_rows(2 * n)
 
     other = 1 + 2 * (1 - core)
     for m in range(2):
@@ -210,15 +230,8 @@
     @pl.loop(0, 2)
     def _(m):
         activate(2 * (1 - core) + m)
-        spread(other + m)
-
-    def term(j, g0, a0, k):
-        return lax.dot_general(
-            gos[pl.ds(pl.multiple_of(g0 * B, B), k), pl.ds(pl.multiple_of(j * 512, 512), 512)],
-            act[pl.ds(pl.multiple_of(a0 * B, B), k), :],
-            TN,
-            preferred_element_type=F32,
-        )
+        centre(other + m)
+        sides(other + m)
 
     def x_copy(j, d):
         to, dev = x_peer(d)
@@ -233,7 +246,7 @@
         return remote(send_z.at[g, to], recv_z.at[g, d - 1], z_s.at[g, d - 1], z_r.at[g, d - 1], dev)
 
     def first_x(j):
-        p = term(j, 1, 0, 4 * B).reshape(8, 2, 32, 256)
+        p = px[j] + term(j, other, 2 * (1 - core), 2 * B).reshape(8, 2, 32, 256)
         px[j] = p
         for a in range(2):
             for b in range(2):
@@ -242,7 +255,7 @@
             x_copy(j, d).start()
 
     def first_y(t, j, g0, a0, k):
-        p = term(j, g0, a0, k).reshape(16, 4, 8, 256)
+        p = py[t] + term(j, g0, a0, k).reshape(16, 4, 8, 256)
         py[t] = p
         for to in range(4):
             send_y[t, to] = p[:, to].reshape(128, 256).astype(BF)
@@ -250,18 +263,18 @@
             y_copy(t, d).start()
 
     def first_z(g, j, g0, a0, k):
-        p = term(j, g0, a0, k).reshape(8, 64, 256)
+        p = pz[g] + term(j, g0, a0, k).reshape(8, 64, 256)
         pz[g] = p
         send_z[g] = p.astype(BF)
         for d in range(1, 8):
             z_copy(g, d).start()
 
-    first_z(0, 2, 1 + xlo, 1 - xlo, 3 * B)
-
     @pl.loop(0, 2)
     def _(j):
-        first_y(j, j, 1 + xlo, 1 - xlo, 3 * B)
-        first_x(j)
+        first_y(j, j, 2 - core + xlo, 2 - core - xlo, 2 * B)
+
+    first_z(0, 2, 2 - core + xlo, 2 - core - xlo, 2 * B)
+    first_x(0)
 
     near = 5 * (1 - xlo)
     half = ext.at[near, pl.ds(pl.multiple_of(16 + 384 * core, 16), 384)]
@@ -269,22 +282,44 @@
     remote(half, half, halo_s.at[0], halo_r, sib).wait_recv()
     forward = remote(half, half, fwd_s, fwd_r, sib)
     forward.start()
-    first_x(2)
+
+    first_x(1)
+
+    def local_pairs(j):
+        return term(j, 2 - xlo, xlo, 3 * B)
+
+    pz[1] = local_pairs(2).reshape(8, 64, 256)
+
+    @pl.loop(0, 2)
+    def _(j):
+        py[2 + j] = local_pairs(j).reshape(16, 4, 8, 256)
 
     for side, at in ((0, 0), (1, 16 + B)):
         edge = ext.at[near, pl.ds(at, 16)]
         remote(edge, edge, hrim_s.at[side, 0], hrim_r.at[side], sib).wait_recv()
     remote(other_half, other_half, fwd_s, fwd_r, sib).wait_recv()
-    spread(near)
-
-    first_z(1, 2, 2 * (1 - xlo), 0, 4 * B)
+    centre(near)
+    sides(near)
 
     @pl.loop(0, 2)
     def _(j):
-        first_y(2 + j, j, 2 * (1 - xlo), 0, 4 * B)
+        first_y(2 + j, j, near, 3 * (1 - xlo), B)
+
+    first_z(1, 2, near, 3 * (1 - xlo), B)
+    first_x(2)
 
     for cp in w_loads:
         cp.wait()
+
+    def own_share(n):
+        m, at = n // 3, lax.rem(n, 3) * 256
+
+        def rows(r):
+            return pl.ds(pl.multiple_of(r * B + at, 256), 256)
+
+        here = lax.dot_general(gos[rows(own + m), :], wv[1], NT, preferred_element_type=F32)
+        there = lax.dot_general(gos[rows(own + 1 - m), :], wv[2 * m], NT, preferred_element_type=F32)
+        acc[pl.ds(pl.multiple_of(n * 256, 256), 256), :] = here + there
 
     @pl.loop(0, 3)
     def _(n):
@@ -453,7 +488,7 @@
     cp.wait_recv()
     total = total + ar_core[...]
     at = 1
-    for stage, (peer, count, slots) in enumerate(((y_peer, 3, ar_y), (x_peer, 3, ar_x), (z_peer, 7, ar_z))):
+    for stage, (peer, count, slots) in enumerate(((plane_peer, 15, ar_xy), (z_peer, 7, ar_z))):
         ar_own[1 + stage] = total
         copies = []
         for d in range(1, count + 1):
@@ -535,17 +570,16 @@
         vmem((4, 2, 8, 128), F32),
         vmem((3, 2, 8, 128), F32),
         vmem((3, 3, 8, 128), F32),
-        vmem((4, 8, 128), F32),
+        vmem((3, 8, 128), F32),
         vmem((8, 128), F32),
-        vmem((3, 8, 128), F32),
-        vmem((3, 8, 128), F32),
+        vmem((15, 8, 128), F32),
         vmem((7, 8, 128), F32),
         dma((4,)), dma((9,)), dma, dma((4,)), dma((4,)), dma((2, 2)), dma((2, 2)),
         dma((2,)), dma, dma((2, 2)), dma((2,)), dma, dma,
         dma((3, 3)), dma((3, 3)), dma((3,)), dma((3,)),
         dma((4, 3)), dma((4, 3)), dma((2, 3)), dma((2, 3)),
         dma((2, 7)), dma((2, 7)), dma((2, 3)), dma((2, 3)),
-        dma((2, 7)), dma((2, 7)), dma((3,)), dma((3,)), dma((14,)), dma((14,)),
+        dma((2, 7)), dma((2, 7)), dma((3,)), dma((3,)), dma((23,)), dma((23,)),
     ]
     grad_in, grad_kernel = pl.pallas_call(
         body,

time: 65.8 us -> 63.5 us (0.965)
  Pallas kernels: 63.3 us -> 61 us
    pallas_call x1, Pallas kernels: 63.3 us -> 61 us  [shards(): pl.pallas_call(body, out_shape=(jax.ShapeDtypeStruct((2, B, C), BF), jax....]
where the time goes in v3:
time: 63.5 us; the launch traced here: 63.4 us
  Pallas kernels  61 us (96%)
  local copies, waits for them, and re-layouts  1.76 us (3%)
  between operations  0.64 us (1%)
    pallas_call x1, Pallas kernels, shards(): pl.pallas_call(body, out_shape=(jax.ShapeDtypeStruct((2, B, C), BF), jax....  61 us
    unnamed x2, local copies, waits for them, and re-layouts  1.76 us

profile of v3, /device:TPU:1, one launch (start us, length us, event | category | flops | bytes accessed | tf_op | source)
XLA Modules:
  0.0 63.4 jit_solution(9938764087897956427)
XLA Ops:
  0.6 61.0 %conv_backward.1 = (bf16[2,768,512]{2,1,0:T(8,128)(2,1)S(1)}, f32[3,3,8,128]{3,2,1,0:T(8,128)S(1)}) custom-call(bf16[2,768,512]{2,1,0:T(8,128)(2,1)} %pre_hbm.1, bf16[2,768,512]{2,1,0:T(8,128)(2,1)} %go_hbm.1, bf16[3,3,512,512]{3,2,1,0:T(8,128)(2,1)} %w_hbm.1), custom_call_target="tpu_custom_call" | custom-call | flops 14499999744 | bytes 12000000 | tf_op jit(solution)/shard_map/conv_backward/pallas_call | solution.py:584
  61.6 1.1 %copy.7 = bf16[2,768,512]{2,1,0:T(8,128)(2,1)} copy(bf16[2,768,512]{2,1,0:T(8,128)(2,1)S(1)} %get-tuple-element.8) | data formatting | bytes 3145728
  62.8 0.6 copy.8

commit v4 on v3

--- a/solution.py
+++ b/solution.py
@@ -225,13 +225,11 @@
     for h in range(2):
         part = pre_half.at[pl.ds(2 * (1 - core), 2), :, pl.ds(128 * h, 128)]
         remote(part, part, sib_s.at[2 + h], sib_r.at[2 + h], sib).wait_recv()
-    wait_rims(1 - core)
 
     @pl.loop(0, 2)
     def _(m):
         activate(2 * (1 - core) + m)
         centre(other + m)
-        sides(other + m)
 
     def x_copy(j, d):
         to, dev = x_peer(d)
@@ -269,10 +267,14 @@
         for d in range(1, 8):
             z_copy(g, d).start()
 
+    first_y(1, 1, 2 - core + xlo, 2 - core - xlo, 2 * B)
+    wait_rims(1 - core)
+
     @pl.loop(0, 2)
-    def _(j):
-        first_y(j, j, 2 - core + xlo, 2 - core - xlo, 2 * B)
-
+    def _(m):
+        sides(other + m)
+
+    first_y(0, 0, 2 - core + xlo, 2 - core - xlo, 2 * B)
     first_z(0, 2, 2 - core + xlo, 2 - core - xlo, 2 * B)
     first_x(0)
 
@@ -415,6 +417,9 @@
         to, dev = x_peer(d)
         return remote(send_xf.at[to], recv_xf.at[d - 1], xf_s.at[d - 1], xf_r.at[d - 1], dev)
 
+    finish_y(1, xlo)
+    finish_z(1)
+
     for d in (1, 2, 3):
         my_copy(d).wait_recv()
 
@@ -427,9 +432,6 @@
 
     for d in range(1, 8):
         zf_copy(0, d).start()
-
-    finish_z(1)
-    finish_y(1, xlo)
 
     @pl.loop(0, 3)
     def _(n):
@@ -478,6 +480,32 @@
         else:
             for gi in range(2):
                 final[2 * gi, 0:2] = total[2 * gi : 2 * gi + 2]
+
+    def drain():
+        for cp in rims + sib_copies:
+            cp.wait_send()
+
+        @pl.when(owner)
+        def _():
+            for cp in halos:
+                cp.wait_send()
+
+        forward.wait_send()
+        for d in (1, 2, 3):
+            for j in range(3):
+                x_copy(j, d).wait_send()
+            for t in range(4):
+                y_copy(t, d).wait_send()
+            for g in range(2):
+                mx_copy(g, d).wait_send()
+                mz_copy(g, d).wait_send()
+            my_copy(d).wait_send()
+            xf_copy(d).wait_send()
+        for d in range(1, 8):
+            for g in range(2):
+                z_copy(g, d).wait_send()
+                zf_copy(g, d).wait_send()
+        store.wait()
 
     all_terms = final[...].reshape(9, 8, 128)
     total = jnp.sum(all_terms * all_terms, axis=0)
@@ -496,10 +524,16 @@
             at = at + 1
             cp.start()
             copies.append(cp)
+        if stage == 0:
+            drain()
+        else:
+            for cp in sums:
+                cp.wait_send()
         for cp in copies:
             cp.wait_recv()
         for d in range(count):
             total = total + slots[d]
+        sums = [] if stage else sums
         sums += copies
     grand = jnp.sum(total)
     factor = jnp.float32(3.0 * C) * lax.rsqrt(jnp.full((8, 128), grand, F32) + 1e-06)
@@ -507,32 +541,8 @@
         for j in range(3):
             gk_ref[i, j] = final[i, j] * factor
 
-    for cp in rims + sib_copies:
-        cp.wait_send()
-
-    @pl.when(owner)
-    def _():
-        for cp in halos:
-            cp.wait_send()
-
-    forward.wait_send()
-    for d in (1, 2, 3):
-        for j in range(3):
-            x_copy(j, d).wait_send()
-        for t in range(4):
-            y_copy(t, d).wait_send()
-        for g in range(2):
-            mx_copy(g, d).wait_send()
-            mz_copy(g, d).wait_send()
-        my_copy(d).wait_send()
-        xf_copy(d).wait_send()
-    for d in range(1, 8):
-        for g in range(2):
-            z_copy(g, d).wait_send()
-            zf_copy(g, d).wait_send()
     for cp in sums:
         cp.wait_send()
-    store.wait()
 
 
 def shards(pre_act, grad_out, kernel):

time: 63.5 us -> 63.1 us (level)
  no operation moved by 1% of the time
where the time goes in v4:
time: 63.1 us; the launch traced here: 63 us
  Pallas kernels  60.6 us (96%)
  local copies, waits for them, and re-layouts  1.76 us (3%)
  between operations  0.64 us (1%)
    pallas_call x1, Pallas kernels, shards(): pl.pallas_call(body, out_shape=(jax.ShapeDtypeStruct((2, B, C), BF), jax....  60.6 us
    unnamed x2, local copies, waits for them, and re-layouts  1.76 us

profile of v4, /device:TPU:1, one launch (start us, length us, event | category | flops | bytes accessed | tf_op | source)
XLA Modules:
  0.0 63.0 jit_solution(3238697756502747300)
XLA Ops:
  0.6 60.6 %conv_backward.1 = (bf16[2,768,512]{2,1,0:T(8,128)(2,1)S(1)}, f32[3,3,8,128]{3,2,1,0:T(8,128)S(1)}) custom-call(bf16[2,768,512]{2,1,0:T(8,128)(2,1)} %pre_hbm.1, bf16[2,768,512]{2,1,0:T(8,128)(2,1)} %go_hbm.1, bf16[3,3,512,512]{3,2,1,0:T(8,128)(2,1)} %w_hbm.1), custom_call_target="tpu_custom_call" | custom-call | flops 14499999744 | bytes 12000000 | tf_op jit(solution)/shard_map/conv_backward/pallas_call | solution.py:594
  61.2 1.1 %copy.7 = bf16[2,768,512]{2,1,0:T(8,128)(2,1)} copy(bf16[2,768,512]{2,1,0:T(8,128)(2,1)S(1)} %get-tuple-element.8) | data formatting | bytes 3145728
  62.4 0.6 copy.8

commit v5 on v4

--- a/solution.py
+++ b/solution.py
@@ -12,6 +12,8 @@
 C = 512
 TN = (((0,), (0,)), ((), ()))
 NT = (((1,), (1,)), ((), ()))
+FAR_Z = (4, 3, 5, 2, 6, 1, 7)
+FAR_XY = (10, 6, 14, 9, 11, 5, 7, 13, 15, 2, 8, 1, 3, 4, 12)
 
 
 def sigmoid(v):
@@ -457,7 +459,7 @@
             for d in range(3):
                 total = total + recv_mx[d, gi, j].astype(F32)
             send_zf[:, 3 + 2 * gi + j] = total.reshape(8, 8, 128)
-    for d in range(1, 8):
+    for d in FAR_Z:
         zf_copy(1, d).start()
 
     @pl.loop(3, 6)
@@ -516,10 +518,10 @@
     cp.wait_recv()
     total = total + ar_core[...]
     at = 1
-    for stage, (peer, count, slots) in enumerate(((plane_peer, 15, ar_xy), (z_peer, 7, ar_z))):
+    for stage, (peer, order, slots) in enumerate(((plane_peer, FAR_XY, ar_xy), (z_peer, FAR_Z, ar_z))):
         ar_own[1 + stage] = total
         copies = []
-        for d in range(1, count + 1):
+        for d in order:
             cp = remote(ar_own.at[1 + stage], slots.at[d - 1], ar_s.at[at], ar_r.at[at], peer(d)[1])
             at = at + 1
             cp.start()
@@ -531,7 +533,7 @@
                 cp.wait_send()
         for cp in copies:
             cp.wait_recv()
-        for d in range(count):
+        for d in range(len(order)):
             total = total + slots[d]
         sums = [] if stage else sums
         sums += copies

time: 63.1 us -> 63 us (level)
  no operation moved by 1% of the time
where the time goes in v5:
time: 63 us; the launch traced here: 62.9 us
  Pallas kernels  60.5 us (96%)
  local copies, waits for them, and re-layouts  1.76 us (3%)
  between operations  0.64 us (1%)
    pallas_call x1, Pallas kernels, shards(): pl.pallas_call(body, out_shape=(jax.ShapeDtypeStruct((2, B, C), BF), jax....  60.5 us
    unnamed x2, local copies, waits for them, and re-layouts  1.76 us

profile of v5, /device:TPU:1, one launch (start us, length us, event | category | flops | bytes accessed | tf_op | source)
XLA Modules:
  0.0 62.9 jit_solution(16184490452682862011)
XLA Ops:
  0.6 60.5 %conv_backward.1 = (bf16[2,768,512]{2,1,0:T(8,128)(2,1)S(1)}, f32[3,3,8,128]{3,2,1,0:T(8,128)S(1)}) custom-call(bf16[2,768,512]{2,1,0:T(8,128)(2,1)} %pre_hbm.1, bf16[2,768,512]{2,1,0:T(8,128)(2,1)} %go_hbm.1, bf16[3,3,512,512]{3,2,1,0:T(8,128)(2,1)} %w_hbm.1), custom_call_target="tpu_custom_call" | custom-call | flops 14499999744 | bytes 12000000 | tf_op jit(solution)/shard_map/conv_backward/pallas_call | solution.py:596
  61.1 1.1 %copy.7 = bf16[2,768,512]{2,1,0:T(8,128)(2,1)} copy(bf16[2,768,512]{2,1,0:T(8,128)(2,1)S(1)} %get-tuple-element.8) | data formatting | bytes 3145728
  62.3 0.6 copy.8
